TPU v7x, 256 devices: a whole 4x4x8 slice. The times are simulated.
256 devices in a mesh: seq: 64 (over z, x, core), head: 4 (over y).
Axes of the slice: x: 4, y: 4, z: 8, core: 2. Of those that a mesh axis runs over, the one named last changes fastest.
Arguments:
- queries: bfloat16 [8192, 4096], P(('seq', 'head')), may hold values from -6 to 6
- keys: bfloat16 [8192, 4096], P(('seq', 'head')), may hold values from -6 to 6
- values: bfloat16 [8192, 4096], P(('seq', 'head')), may hold values from -6 to 6
- grad_out: bfloat16 [8192, 4096], P(('seq', 'head')), may hold values from -6 to 6
- random_blocks: int32 [32, 128, 3], replicated, may hold values from 0 to 127, as said below
- global_blocks: int32 [2], replicated, may hold values from 0 to 127
Outputs:
- attended: bfloat16 [8192, 4096], P(('seq', 'head'))
- grad_queries: bfloat16 [8192, 4096], P(('seq', 'head'))
- grad_keys: bfloat16 [8192, 4096], P(('seq', 'head'))
- grad_values: bfloat16 [8192, 4096], P(('seq', 'head'))
Inputs may be any that keep to these rules, and one draw needn't show every extreme that they name: `random_blocks`: for the heads of one index of head and the query blocks of one index of seq, at most 2 random entries lie in the blocks of any one index of seq, and in every such group some index of seq holds exactly 2.
All inputs are finite; a program needn't handle non-finite values.
Results may differ from a plain program's by a relative error of at most 0.034.
Values may be sent and summed in bfloat16 or wider, within the bound.
A program may use at most 128 MiB of HBM per device.

v0:
```python
import jax
import jax.numpy as jnp
from jax import lax
from jax.sharding import PartitionSpec as P

HEAD_DIM = 128
BLOCK = 64
RAND_BLOCKS = 3
GLOB_BLOCKS = 2


def extended(shard, sides, width):
    for axis, dim in sides:
        devices, length = (lax.axis_size(axis), shard.shape[dim])
        up = [(i, (i + 1) % devices) for i in range(devices - 1)]
        down = [(j, i) for i, j in up]
        last = lax.slice_in_dim(shard, length - width, length, axis=dim)
        first = lax.slice_in_dim(shard, 0, width, axis=dim)
        before = lax.ppermute(last, axis, up)
        after = lax.ppermute(first, axis, down)
        shard = jnp.concatenate([before, shard, after], axis=dim)
    return shard


def spread_2(shard, axis, root):
    mine = lax.axis_index(axis) == root
    return lax.psum(jnp.where(mine, shard, jnp.zeros_like(shard)), axis)


def product(formula, former, latter):
    return jnp.einsum(formula, former, latter, preferred_element_type=jnp.float32)


def spread(near_part, offset):
    widths = [(0, 0), (offset, 2 - offset), (0, 0), (0, 0), (0, 0)]
    return jnp.pad(near_part, widths)


def body(queries, keys, values, grad_out, random_blocks, global_blocks):
    score_scale = HEAD_DIM ** (-0.5)
    query_rows, key_rows, value_rows, upstream_rows = (
        lax.all_to_all(queries, "head", split_axis=1, concat_axis=0, tiled=True),
        lax.all_to_all(keys, "head", split_axis=1, concat_axis=0, tiled=True),
        lax.all_to_all(values, "head", split_axis=1, concat_axis=0, tiled=True),
        lax.all_to_all(grad_out, "head", split_axis=1, concat_axis=0, tiled=True),
    )
    tokens_here, width_here = query_rows.shape
    heads_here = width_here // HEAD_DIM
    blocks_here = tokens_here // BLOCK
    shards = lax.axis_size("seq")
    my_shard = lax.axis_index("seq")
    my_group = lax.axis_index("head")
    tile_shape = (blocks_here, BLOCK, heads_here, HEAD_DIM)
    query_tiles = query_rows.reshape(tile_shape)
    incoming_gradient = upstream_rows.reshape(tile_shape)
    pair_rows = jnp.stack([key_rows, value_rows])
    widened = extended(pair_rows, (("seq", 1),), BLOCK)
    widened = widened.reshape((2, blocks_here + 2) + tile_shape[1:])
    window = jnp.stack([widened[:, :-2], widened[:, 1:-1], widened[:, 2:]], axis=2)
    total_blocks = shards * blocks_here
    block_ids = my_shard * blocks_here + jnp.arange(blocks_here, dtype=jnp.int32)
    window_ok = jnp.stack([block_ids >= 1, block_ids >= 0, block_ids + 1 < total_blocks], axis=1)
    pair_tiles = pair_rows.reshape((2,) + tile_shape)
    fetched = []
    for glob_index in range(GLOB_BLOCKS):
        target = global_blocks[glob_index]
        global_tile = lax.dynamic_index_in_dim(pair_tiles, target % blocks_here, 1, keepdims=False)
        fetched.append(spread_2(global_tile, "seq", target // blocks_here))
    global_pair = jnp.stack(fetched, axis=1)
    requests = heads_here * blocks_here * RAND_BLOCKS
    slot_count = max(2, requests // shards + 1)
    request_table = lax.dynamic_slice_in_dim(random_blocks, my_group * heads_here, heads_here, 0)
    request_table = (
        request_table.reshape(heads_here, shards, blocks_here, RAND_BLOCKS)
        .transpose(1, 0, 2, 3)
        .reshape(shards, requests)
    )
    owners = request_table // blocks_here
    positions = jnp.arange(requests, dtype=jnp.int32)
    tile_ids = positions // (blocks_here * RAND_BLOCKS) * blocks_here + request_table % blocks_here
    to_me = (owners == my_shard).astype(jnp.int32)
    order_out = jnp.cumsum(to_me, axis=1) - to_me
    slot_ids = jnp.arange(slot_count, dtype=jnp.int32)
    chosen = (to_me[:, None, :] == 1) & (order_out[:, None, :] == slot_ids[None, :, None])
    slot_used = jnp.any(chosen, axis=2)
    send_ids = jnp.sum(jnp.where(chosen, tile_ids[:, None, :], 0), axis=2)
    send_block = send_ids % blocks_here
    send_head = send_ids // blocks_here
    slot_mask = slot_used[:, :, None, None]
    key_send = jnp.where(
        slot_mask, pair_tiles[0][send_block, :, send_head, :], jnp.zeros((), jnp.bfloat16)
    )
    value_send = jnp.where(
        slot_mask, pair_tiles[1][send_block, :, send_head, :], jnp.zeros((), jnp.bfloat16)
    )
    key_recv, value_recv = (
        lax.all_to_all(key_send, "seq", split_axis=0, concat_axis=0, tiled=True),
        lax.all_to_all(value_send, "seq", split_axis=0, concat_axis=0, tiled=True),
    )
    my_table = lax.dynamic_index_in_dim(request_table, my_shard, 0, keepdims=False)
    my_owner = my_table // blocks_here
    by_owner = (my_owner[:, None] == jnp.arange(shards, dtype=jnp.int32)[None, :]).astype(jnp.int32)
    my_slot = jnp.sum((jnp.cumsum(by_owner, axis=0) - by_owner) * by_owner, axis=1)
    rand_shape = (heads_here, blocks_here, RAND_BLOCKS, BLOCK, HEAD_DIM)
    rand_keys = key_recv[my_owner, my_slot].reshape(rand_shape)
    rand_values = value_recv[my_owner, my_slot].reshape(rand_shape)
    attention_logits = (
        jnp.concatenate(
            [
                product("iahd,ijbhd->hiajb", query_tiles, window[0]),
                product("iahd,jbhd->hiajb", query_tiles, global_pair[0]),
                product("iahd,hijbd->hiajb", query_tiles, rand_keys),
            ],
            axis=3,
        )
        * score_scale
    )
    key_valid = jnp.concatenate(
        [window_ok, jnp.ones((blocks_here, GLOB_BLOCKS + RAND_BLOCKS), bool)], axis=1
    )
    attention_logits = jnp.where(key_valid[None, :, None, :, None], attention_logits, -jnp.inf)
    row_max = jnp.max(attention_logits, axis=(3, 4), keepdims=True)
    exponent = jnp.exp(attention_logits - row_max)
    row_sum = jnp.sum(exponent, axis=(3, 4), keepdims=True)
    probability = exponent / row_sum
    attention_weight = probability.astype(jnp.bfloat16)
    split_at = 3 + GLOB_BLOCKS
    weight_win = attention_weight[:, :, :, :3]
    weight_glob = attention_weight[:, :, :, 3:split_at]
    weight_rand = attention_weight[:, :, :, split_at:]
    mixed = product("hiajb,ijbhd->iahd", weight_win, window[1])
    mixed = mixed + product("hiajb,jbhd->iahd", weight_glob, global_pair[1])
    mixed = mixed + product("hiajb,hijbd->iahd", weight_rand, rand_values)
    attended = mixed.astype(jnp.bfloat16)
    out_rows = attended.reshape(tokens_here, width_here)
    row_delta = jnp.sum(
        incoming_gradient.astype(jnp.float32) * attended.astype(jnp.float32), axis=3
    ).transpose(2, 0, 1)[:, :, :, None, None]
    probability_gradient = jnp.concatenate(
        [
            product("iahd,ijbhd->hiajb", incoming_gradient, window[1]),
            product("iahd,jbhd->hiajb", incoming_gradient, global_pair[1]),
            product("iahd,hijbd->hiajb", incoming_gradient, rand_values),
        ],
        axis=3,
    )
    logit_gradient = (probability * (probability_gradient - row_delta)).astype(jnp.bfloat16)
    grad_win = logit_gradient[:, :, :, :3]
    grad_glob = logit_gradient[:, :, :, 3:split_at]
    grad_rand = logit_gradient[:, :, :, split_at:]
    query_gradient = product("hiajb,ijbhd->iahd", grad_win, window[0])
    query_gradient = query_gradient + product("hiajb,jbhd->iahd", grad_glob, global_pair[0])
    query_gradient = query_gradient + product("hiajb,hijbd->iahd", grad_rand, rand_keys)
    query_gradient = (
        (score_scale * query_gradient).astype(jnp.bfloat16).reshape(tokens_here, width_here)
    )
    near_grads = jnp.stack(
        [
            score_scale * product("hiajb,iahd->ijbhd", grad_win, query_tiles),
            product("hiajb,iahd->ijbhd", weight_win, incoming_gradient),
        ]
    )
    accum = (
        spread(near_grads[:, :, 1], 1)
        + spread(near_grads[:, :, 0], 0)
        + spread(near_grads[:, :, 2], 2)
    )
    rim_rows = jnp.concatenate([accum[:, :1], accum[:, -1:]], axis=1).reshape(
        2, 2 * BLOCK, width_here
    )
    arrived = extended(rim_rows.astype(jnp.bfloat16), (("seq", 1),), BLOCK).astype(rim_rows.dtype)
    arrived = arrived.reshape(2, 4, BLOCK, heads_here, HEAD_DIM)
    own_blocks = accum[:, 1:-1]
    own_blocks = own_blocks.at[:, 0].add(arrived[:, 0]).at[:, -1].add(arrived[:, 3])
    far_keys = score_scale * product("hiajb,iahd->jbhd", grad_glob, query_tiles)
    far_values = product("hiajb,iahd->jbhd", weight_glob, incoming_gradient)
    sum_keys, sum_values = lax.psum((far_keys, far_values), "seq")
    for glob_index in range(GLOB_BLOCKS):
        target = global_blocks[glob_index]
        owner_flag = (target // blocks_here == my_shard).astype(jnp.float32)
        addition = jnp.stack([sum_keys[glob_index], sum_values[glob_index]]) * owner_flag
        own_blocks = own_blocks.at[:, target % blocks_here].add(addition)
    tile_zero = jnp.zeros((shards, slot_count, BLOCK, HEAD_DIM), jnp.bfloat16)
    rand_grad_keys = (
        (score_scale * product("hiajb,iahd->hijbd", grad_rand, query_tiles))
        .astype(jnp.bfloat16)
        .reshape(requests, BLOCK, HEAD_DIM)
    )
    rand_grad_values = (
        product("hiajb,iahd->hijbd", weight_rand, incoming_gradient)
        .astype(jnp.bfloat16)
        .reshape(requests, BLOCK, HEAD_DIM)
    )
    keys_box = tile_zero.at[my_owner, my_slot].set(rand_grad_keys)
    values_box = tile_zero.at[my_owner, my_slot].set(rand_grad_values)
    back_keys, back_values = (
        lax.all_to_all(keys_box, "seq", split_axis=0, concat_axis=0, tiled=True),
        lax.all_to_all(values_box, "seq", split_axis=0, concat_axis=0, tiled=True),
    )
    selector = (
        (
            send_ids[:, :, None]
            == jnp.arange(heads_here * blocks_here, dtype=jnp.int32)[None, None, :]
        )
        & slot_used[:, :, None]
    ).astype(jnp.bfloat16)

    def collect(returned):
        summed = product("ncs,ncbd->sbd", selector, returned)
        return summed.reshape(heads_here, blocks_here, BLOCK, HEAD_DIM).transpose(1, 2, 0, 3)

    grad_key = (
        (own_blocks[0] + collect(back_keys)).astype(jnp.bfloat16).reshape(tokens_here, width_here)
    )
    grad_value = (
        (own_blocks[1] + collect(back_values)).astype(jnp.bfloat16).reshape(tokens_here, width_here)
    )
    return (
        lax.all_to_all(out_rows, "head", split_axis=0, concat_axis=1, tiled=True),
        lax.all_to_all(query_gradient, "head", split_axis=0, concat_axis=1, tiled=True),
        lax.all_to_all(grad_key, "head", split_axis=0, concat_axis=1, tiled=True),
        lax.all_to_all(grad_value, "head", split_axis=0, concat_axis=1, tiled=True),
    )


def solution(mesh):
    placed = (
        P(("seq", "head"), None),
        P(("seq", "head"), None),
        P(("seq", "head"), None),
        P(("seq", "head"), None),
        P(),
        P(),
    )
    return jax.shard_map(
        body,
        mesh=mesh,
        in_specs=placed,
        out_specs=(
            P(("seq", "head"), None),
            P(("seq", "head"), None),
            P(("seq", "head"), None),
            P(("seq", "head"), None),
        ),
        check_vma=False,
    )
```

profile of v0, /device:TPU:2, one launch (start us, length us, event | category | flops | bytes accessed | tf_op | source)
XLA Modules:
  0.0 680.3 jit_solution(14771707569633310795)
XLA Ops:
  7.2 1.7 copy.551
  8.9 4.5 all-to-all-start.1
  13.9 1.7 copy.552
  15.6 4.5 all-to-all-done.1
  20.1 3.4 all-to-all-start
  24.7 5.4 all-to-all-done
  30.1 4.0 all-to-all-start.6
  37.3 2.3 gather_fusion
  39.6 1.3 all-to-all-done.6
  40.9 3.4 all-to-all-start.2
  44.3 3.9 broadcast_select_fusion
  48.3 2.7 all-to-all-done.2
  51.7 12.0 %all-to-all-start.3 = ((bf16[64,2,64,128]{3,2,1,0:T(8,128)(2,1)}), bf16[64,2,64,128]{3,2,1,0:T(8,128)(2,1)S(1)}, u32[]{:S(2)}, u32[]{:S(2)}) async-start(bf16[64,2,64,128]{3,2,1,0:T(8,128)(2,1)} %get-tuple-element.91), calls=%async_computation.3 | async-start | bytes 4194304 | tf_op jit(solution)/shard_map/all_to_all | solution.py:97
  72.0 2.0 collective-permute-start.1
  74.1 2.3 collective-permute-start
  77.2 37.8 %all-to-all-done.3 = bf16[64,2,64,128]{3,2,1,0:T(8,128)(2,1)S(1)} async-done(((bf16[64,2,64,128]{3,2,1,0:T(8,128)(2,1)}), bf16[64,2,64,128]{3,2,1,0:T(8,128)(2,1)S(1)}, u32[]{:S(2)}, u32[]{:S(2)}) %all-to-all-start.3) | async-done | bytes 2097184 | tf_op jit(solution)/shard_map/all_to_all | solution.py:97
  115.0 1.3 copy-done.21
  116.4 5.6 all-to-all-start.4
  123.0 1.9 dynamic-slice_select_fusion
  128.4 186.7 %all-reduce.10.cloned.1.call-done = (bf16[2,1,64,8,128]{4,2,1,3,0:T(8,128)(2,1)}, bf16[2,1,64,8,128]{4,2,1,3,0:T(8,128)(2,1)}) async-done(((bf16[2,1,64,8,128]{4,2,1,3,0:T(8,128)(2,1)}, bf16[2,1,64,8,128]{4,2,1,3,0:T(8,128)(2,1)}), (bf16[2,1,64,8,128]{4,2,1,3,0:T(8,128)(2,1)}, bf16[2,1,64,8,128]{4,2,1,3,0:T(8,128)(2,1)})) %all-reduce.10.cloned.1.call-update) | async-done | bytes 524304 | tf_op jit(solution)/shard_map/psum | solution.py:27
  317.9 1.6 convolution_bitcast_fusion.6
  319.8 3.4 gather_fusion.1
  323.2 1.6 convolution_bitcast_fusion.3
  328.1 1.3 copy-done.6
  329.4 1.3 convolution_convert_fusion
  330.7 1.9 broadcast_in_dim.44.clone
  332.6 7.5 %scatter_fusion.1 = bf16[64,2,64,128]{3,2,1,0:T(8,128)(2,1)} fusion(bf16[64,2,64,128]{3,2,1,0:T(8,128)(2,1)} %broadcast_in_dim.44.clone, s32[48]{0:T(128)S(1)} %get-tuple-element.92, bf16[48,64,128]{2,1,0:T(8,128)(2,1)} %bitcast.339), kind=kCustom, calls=%fused_computation.5 | custom fusion | bytes 2359680 | tf_op jit(solution)/shard_map/scatter | solution.py:195
  340.1 5.1 copy.382
  345.2 7.2 %all-to-all-start.10 = ((bf16[64,2,64,128]{3,1,2,0:T(2,128)(2,1)}), bf16[64,2,64,128]{3,1,2,0:T(2,128)(2,1)}, u32[]{:S(2)}, u32[]{:S(2)}) async-start(bf16[64,2,64,128]{3,1,2,0:T(2,128)(2,1)} %copy.382), calls=%async_computation.10 | async-start | bytes 4194304 | tf_op jit(solution)/shard_map/all_to_all | solution.py:198
  353.2 2.5 convolution_bitcast_fusion.5
  355.7 1.3 slice_bitcast_fusion
  357.0 1.5 convolution_bitcast_fusion.2
  358.5 3.4 gather_fusion.3
  361.9 1.6 fusion.99
  365.0 2.2 multiply_reduce_fusion
  367.6 1.7 fusion.2
  369.3 1.3 copy-done.7
  370.9 1.8 broadcast_in_dim.44.clone.1
  372.8 6.8 scatter_fusion
  379.6 5.3 copy.375
  385.8 1.5 multiply_bitcast_fusion
  387.4 16.1 %all-to-all-done.10 = bf16[64,2,64,128]{3,1,2,0:T(2,128)(2,1)} async-done(((bf16[64,2,64,128]{3,1,2,0:T(2,128)(2,1)}), bf16[64,2,64,128]{3,1,2,0:T(2,128)(2,1)}, u32[]{:S(2)}, u32[]{:S(2)}) %all-to-all-start.10) | async-done | bytes 2097184 | tf_op jit(solution)/shard_map/all_to_all | solution.py:198
  403.5 5.6 all-to-all-start.8
  409.2 1.6 convolution_bitcast_fusion
  411.2 1.8 fusion.95
  414.3 2.1 convert_element_type.79
  416.4 2.0 fusion.102
  418.3 2.0 collective-permute-start.3
  420.4 2.6 collective-permute-start.2
  423.0 1.6 convolution_bitcast_fusion.9
  425.5 2.1 convolution_bitcast_fusion.7
  429.7 1.3 slice.300
  432.1 1.4 maximum_convert_fusion
  435.5 188.6 %all-reduce.8.cloned.1.call-done = (f32[2,64,8,128]{3,1,2,0:T(8,128)}, f32[2,64,8,128]{3,1,2,0:T(8,128)}) async-done(((f32[2,64,8,128]{3,1,2,0:T(8,128)}, f32[2,64,8,128]{3,1,2,0:T(8,128)}), (f32[2,64,8,128]{3,1,2,0:T(8,128)}, f32[2,64,8,128]{3,1,2,0:T(8,128)})) %all-reduce.8.cloned.1.call-update) | async-done | bytes 1048592 | tf_op jit(solution)/shard_map/psum | solution.py:177
  627.7 3.9 fusion.5
  631.6 4.3 all-to-all-start.5
  635.9 3.9 fusion.7
  639.8 2.8 all-to-all-done.5
  642.5 3.4 all-to-all-start.7
  647.4 5.3 all-to-all-done.7
  652.6 3.4 all-to-all-start.9
  657.0 5.7 all-to-all-done.9
  662.7 3.4 all-to-all-start.11
  668.2 4.5 all-to-all-done.11
  (178 shorter events, 40.5 us)
Async XLA Ops:
  7.2 6.2 copy-start
  7.2 16.4 %copy-start.36 = (bf16[32,4096]{1,0:T(8,128)(2,1)S(1)}, bf16[32,4096]{1,0:T(8,128)(2,1)}, u32[]{:S(2)}) copy-start(bf16[32,4096]{1,0:T(8,128)(2,1)} %param.17) | copy-start | bytes 786436
  7.2 27.4 %copy-start.37 = (bf16[32,4096]{1,0:T(8,128)(2,1)S(1)}, bf16[32,4096]{1,0:T(8,128)(2,1)}, u32[]{:S(2)}) copy-start(bf16[32,4096]{1,0:T(8,128)(2,1)} %param.14) | copy-start | bytes 786436
  8.9 11.1 %all-to-all-start.1 = ((bf16[32,4,1024]{2,0,1:T(8,128)(2,1)}), bf16[32,4,1024]{2,0,1:T(8,128)(2,1)S(1)}, u32[]{:S(2)}, u32[]{:S(2)}) async-start(bf16[32,4,1024]{2,0,1:T(8,128)(2,1)} %bitcast.318), calls=%async_computation.1 | async-start | bytes 524288 | tf_op jit(solution)/shard_map/all_to_all | solution.py:44
  20.1 10.1 %all-to-all-start = ((bf16[32,4,1024]{2,0,1:T(8,128)(2,1)}), bf16[32,4,1024]{2,0,1:T(8,128)(2,1)S(1)}, u32[]{:S(2)}, u32[]{:S(2)}) async-start(bf16[32,4,1024]{2,0,1:T(8,128)(2,1)} %bitcast.319), calls=%async_computation | async-start | bytes 524288 | tf_op jit(solution)/shard_map/all_to_all | solution.py:43
  30.1 10.8 %all-to-all-start.6 = ((bf16[32,4,1024]{2,0,1:T(8,128)(2,1)}), bf16[32,4,1024]{2,0,1:T(8,128)(2,1)}, u32[]{:S(2)}, u32[]{:S(2)}) async-start(bf16[32,4,1024]{2,0,1:T(8,128)(2,1)} %bitcast.316), calls=%async_computation.6 | async-start | bytes 524288 | tf_op jit(solution)/shard_map/all_to_all | solution.py:45
  35.5 0.7 copy-start.30
  40.9 10.1 %all-to-all-start.2 = ((bf16[32,4,1024]{2,0,1:T(8,128)(2,1)}), bf16[32,4,1024]{2,0,1:T(8,128)(2,1)S(1)}, u32[]{:S(2)}, u32[]{:S(2)}) async-start(bf16[32,4,1024]{2,0,1:T(8,128)(2,1)} %bitcast.355), calls=%async_computation.2 | async-start | bytes 524288 | tf_op jit(solution)/shard_map/all_to_all | solution.py:42
  51.0 0.7 copy-start.35
  51.0 12.7 %copy-start.38 = (s32[2]{0:T(128)S(1)}, s32[2]{0:T(128)}, u32[]{:S(2)}) copy-start(s32[2]{0:T(128)} %param.19) | copy-start | bytes 28
  51.7 63.3 %all-to-all-start.3 = ((bf16[64,2,64,128]{3,2,1,0:T(8,128)(2,1)}), bf16[64,2,64,128]{3,2,1,0:T(8,128)(2,1)S(1)}, u32[]{:S(2)}, u32[]{:S(2)}) async-start(bf16[64,2,64,128]{3,2,1,0:T(8,128)(2,1)} %get-tuple-element.91), calls=%async_computation.3 | async-start | bytes 4194304 | tf_op jit(solution)/shard_map/all_to_all | solution.py:97
  63.8 12.7 %copy-start.31 = (bf16[16,8,8,128]{3,2,1,0:T(8,128)(2,1)S(1)}, bf16[16,8,8,128]{3,2,1,0:T(8,128)(2,1)}, u32[]{:S(2)}) copy-start(bf16[16,8,8,128]{3,2,1,0:T(8,128)(2,1)} %copy-done.30) | copy-start | bytes 786436
  71.2 5.2 copy-start.33
  72.0 54.6 %collective-permute-start.1 = (bf16[2,64,1024]{2,1,0:T(8,128)(2,1)}, bf16[2,64,1024]{2,1,0:T(8,128)(2,1)}, u32[]{:S(2)}, u32[]{:S(2)}) collective-permute-start(bf16[2,64,1024]{2,1,0:T(8,128)(2,1)} %get-tuple-element.87), channel_id=1, source_target_pairs={{4,0},{8,4},{12,8},{16,12},{20,16},{24,20},{28,24},{32,28},{36,32}... | collective-permute-start | bytes 786440 | tf_op jit(solution)/shard_map/ppermute | solution.py:20
  74.1 52.6 %collective-permute-start = (bf16[2,64,1024]{2,1,0:T(8,128)(2,1)}, bf16[2,64,1024]{2,1,0:T(8,128)(2,1)}, u32[]{:S(2)}, u32[]{:S(2)}) collective-permute-start(bf16[2,64,1024]{2,1,0:T(8,128)(2,1)} %get-tuple-element.86), channel_id=1, source_target_pairs={{0,4},{4,8},{8,12},{12,16},{16,20},{20,24},{24,28},{28,32},{32,36}... | collective-permute-start | bytes 786440 | tf_op jit(solution)/shard_map/ppermute | solution.py:19
  115.0 1.3 copy-start.21
  116.4 228.8 %all-to-all-start.4 = ((bf16[64,2,64,128]{3,2,1,0:T(8,128)(2,1)}), bf16[64,2,64,128]{3,2,1,0:T(8,128)(2,1)}, u32[]{:S(2)}, u32[]{:S(2)}) async-start(bf16[64,2,64,128]{3,2,1,0:T(8,128)(2,1)} %get-tuple-element.90), calls=%async_computation.4 | async-start | bytes 4194304 | tf_op jit(solution)/shard_map/all_to_all | solution.py:98
  122.0 193.1 %all-reduce.10.cloned.1.call-start = ((), (), s32[]{:S(2)}) async-start(), calls=%async_computation.13 | async-start | bytes 1048576 | tf_op jit(solution)/shard_map/psum | solution.py:27
  125.8 2.2 copy-start.27
  317.1 0.8 copy-start.22
  317.9 1.6 copy-start.4
  323.2 1.6 copy-start.2
  326.8 2.6 copy-start.9
  328.1 1.3 copy-start.6
  345.1 7.4 %copy-start.39 = (s32[5]{0:T(128)S(1)}, s32[5]{0:T(128)}, u32[]{:S(2)}) copy-start(s32[5]{0:T(128)} %constant.247.clone.1) | copy-start | bytes 64
  345.2 58.4 %all-to-all-start.10 = ((bf16[64,2,64,128]{3,1,2,0:T(2,128)(2,1)}), bf16[64,2,64,128]{3,1,2,0:T(2,128)(2,1)}, u32[]{:S(2)}, u32[]{:S(2)}) async-start(bf16[64,2,64,128]{3,1,2,0:T(2,128)(2,1)} %copy.382), calls=%async_computation.10 | async-start | bytes 4194304 | tf_op jit(solution)/shard_map/all_to_all | solution.py:198
  352.5 3.1 copy-start.5
  353.2 3.8 copy-start.10
  361.9 1.7 copy-start.17
  361.9 2.1 copy-start.26
  363.5 1.0 copy-start.16
  363.5 1.4 copy-start.23
  363.5 1.4 copy-start.28
  364.0 3.2 copy-start.11
  365.0 2.6 copy-start.3
  365.0 2.6 copy-start.18
  365.0 2.6 copy-start.20
  369.3 1.3 copy-start.7
  379.5 5.3 copy-start.8
  385.8 17.7 %copy-start.14 = (bf16[8,2,64,3,64]{2,4,3,1,0:T(8,128)(2,1)}, bf16[8,2,64,3,64]{2,4,3,1,0:T(8,128)(2,1)S(1)}, u32[]{:S(2)}) copy-start(bf16[8,2,64,3,64]{2,4,3,1,0:T(8,128)(2,1)S(1)} %get-tuple-element.67) | copy-start | bytes 1179652
  387.4 21.8 %copy-start.12 = (bf16[2,64,8,128,1]{3,2,1,0,4:T(8,128)(2,1)S(1)}, bf16[2,64,8,128,1]{3,2,1,0,4:T(8,128)(2,1)}, u32[]{:S(2)}) copy-start(bf16[2,64,8,128,1]{3,2,1,0,4:T(8,128)(2,1)} %bitcast_bitcast_fusion) | copy-start | bytes 786436
  403.5 228.1 %all-to-all-start.8 = ((bf16[64,2,64,128]{3,1,2,0:T(2,128)(2,1)}), bf16[64,2,64,128]{3,1,2,0:T(2,128)(2,1)}, u32[]{:S(2)}, u32[]{:S(2)}) async-start(bf16[64,2,64,128]{3,1,2,0:T(2,128)(2,1)} %copy.375), calls=%async_computation.8 | async-start | bytes 4194304 | tf_op jit(solution)/shard_map/all_to_all | solution.py:197
  409.1 214.9 %all-reduce.8.cloned.1.call-start = ((), (), s32[]{:S(2)}) async-start(), calls=%async_computation.12 | async-start | bytes 2097152 | tf_op jit(solution)/shard_map/psum | solution.py:177
  409.2 1.6 copy-start.19
  413.1 9.8 %copy-start.13 = (bf16[48,64,128]{2,1,0:T(8,128)(2,1)S(1)}, bf16[48,64,128]{2,1,0:T(8,128)(2,1)}, u32[]{:S(2)}) copy-start(bf16[48,64,128]{2,1,0:T(8,128)(2,1)} %gather_fusion.1) | copy-start | bytes 2359300
  416.4 8.2 %copy-start.15 = (bf16[8,2,64,3,64]{2,4,3,1,0:T(8,128)(2,1)S(1)}, bf16[8,2,64,3,64]{2,4,3,1,0:T(8,128)(2,1)}, u32[]{:S(2)}) copy-start(bf16[8,2,64,3,64]{2,4,3,1,0:T(8,128)(2,1)} %copy-done.14) | copy-start | bytes 1179652
  416.4 8.2 %copy-start.25 = (bf16[2,3,64,8,128]{4,2,1,0,3:T(8,128)(2,1)S(1)}, bf16[2,3,64,8,128]{4,2,1,0,3:T(8,128)(2,1)}, u32[]{:S(2)}) copy-start(bf16[2,3,64,8,128]{4,2,1,0,3:T(8,128)(2,1)} %get-tuple-element.71) | copy-start | bytes 2359300
  418.3 13.8 %collective-permute-start.3 = (bf16[2,64,1024]{2,1,0:T(8,128)(2,1)}, bf16[2,64,1024]{2,1,0:T(8,128)(2,1)}, u32[]{:S(2)}, u32[]{:S(2)}) collective-permute-start(bf16[2,64,1024]{2,1,0:T(8,128)(2,1)} %get-tuple-element.85), channel_id=1, source_target_pairs={{4,0},{8,4},{12,8},{16,12},{20,16},{24,20},{28,24},{32,28},{36,32}... | collective-permute-start | bytes 786440 | tf_op jit(solution)/shard_map/ppermute | solution.py:20
  420.4 11.8 %collective-permute-start.2 = (bf16[2,64,1024]{2,1,0:T(8,128)(2,1)}, bf16[2,64,1024]{2,1,0:T(8,128)(2,1)}, u32[]{:S(2)}, u32[]{:S(2)}) collective-permute-start(bf16[2,64,1024]{2,1,0:T(8,128)(2,1)} %get-tuple-element.84), channel_id=1, source_target_pairs={{0,4},{4,8},{8,12},{12,16},{16,20},{20,24},{24,28},{28,32},{32,36}... | collective-permute-start | bytes 786440 | tf_op jit(solution)/shard_map/ppermute | solution.py:19
  422.9 2.1 copy-start.24
  424.6 1.0 copy-start.29
  425.0 2.6 copy-start.32
  427.7 3.3 copy-start.34
  631.6 11.0 %all-to-all-start.5 = ((bf16[4,32,1024]{2,1,0:T(8,128)(2,1)}), bf16[4,32,1024]{2,1,0:T(8,128)(2,1)S(1)}, u32[]{:S(2)}, u32[]{:S(2)}) async-start(bf16[4,32,1024]{2,1,0:T(8,128)(2,1)} %all_to_all.127), calls=%async_computation.5 | async-start | bytes 524288 | tf_op jit(solution)/shard_map/all_to_all | solution.py:219
  642.5 10.1 %all-to-all-start.7 = ((bf16[4,32,1024]{2,1,0:T(8,128)(2,1)}), bf16[4,32,1024]{2,1,0:T(8,128)(2,1)S(1)}, u32[]{:S(2)}, u32[]{:S(2)}) async-start(bf16[4,32,1024]{2,1,0:T(8,128)(2,1)} %all_to_all.134), calls=%async_computation.7 | async-start | bytes 524288 | tf_op jit(solution)/shard_map/all_to_all | solution.py:220
  646.5 26.9 %copy-start.1 = (s32[32,128,3]{1,0,2:T(8,128)S(1)}, s32[32,128,3]{1,0,2:T(8,128)}, u32[]{:S(2)}) copy-start(s32[32,128,3]{1,0,2:T(8,128)} %param.18) | copy-start | bytes 147460
  652.6 10.1 %all-to-all-start.9 = ((bf16[4,32,1024]{2,1,0:T(8,128)(2,1)}), bf16[4,32,1024]{2,1,0:T(8,128)(2,1)S(1)}, u32[]{:S(2)}, u32[]{:S(2)}) async-start(bf16[4,32,1024]{2,1,0:T(8,128)(2,1)} %all_to_all.139), calls=%async_computation.9 | async-start | bytes 524288 | tf_op jit(solution)/shard_map/all_to_all | solution.py:221
  662.7 10.1 %all-to-all-start.11 = ((bf16[4,32,1024]{2,1,0:T(8,128)(2,1)}), bf16[4,32,1024]{2,1,0:T(8,128)(2,1)S(1)}, u32[]{:S(2)}, u32[]{:S(2)}) async-start(bf16[4,32,1024]{2,1,0:T(8,128)(2,1)} %all_to_all.144), calls=%async_computation.11 | async-start | bytes 524288 | tf_op jit(solution)/shard_map/all_to_all | solution.py:222
Sparse Core Ops, SparseCore 0:
  127.0 188.1 all-reduce.9
  432.2 191.7 all-reduce.7
where the time goes:
time: 683 us; the launch traced here: 680 us
  waiting for transfers between devices  461 us (67%)
  local copies, waits for them, and re-layouts  78.9 us (12%)
  starting transfers between devices  69.4 us (10%)
  matrix products  29 us (4%)
  other arithmetic  21.3 us (3%)
  between operations  20.2 us (3%)
    psum x1, waiting for transfers between devices, body(): sum_keys, sum_values = lax.psum((far_keys, far_values), 'seq')  189 us
    psum x1, waiting for transfers between devices, spread_2(): return lax.psum(jnp.where(mine, shard, jnp.zeros_like(shard)), axis)  187 us
    all_to_all x1, waiting for transfers between devices, body(): lax.all_to_all(key_send, 'seq', split_axis=0, concat_axis=0, tiled=True)  37.8 us
    dot_general x20, matrix products, product(): jnp.einsum(formula, former, latter, preferred_element_type=jnp.float32)  29 us
    all_to_all x1, waiting for transfers between devices, body(): lax.all_to_all(values_box, 'seq', split_axis=0, concat_axis=0, tiled=True)  16.1 us
  transfers between devices with their start and end apart: 18, of which 12 were waited for; matrix products, arithmetic and copies ran while one was open for 17% of the time, Pallas kernels for 0%

commit v1 on v0

--- a/solution.py
+++ b/solution.py
@@ -24,7 +24,7 @@
 
 def spread_2(shard, axis, root):
     mine = lax.axis_index(axis) == root
-    return lax.psum(jnp.where(mine, shard, jnp.zeros_like(shard)), axis)
+    return jnp.sum(lax.all_gather(jnp.where(mine, shard, jnp.zeros_like(shard)), axis), axis=0)
 
 
 def product(formula, former, latter):

time: 683 us -> 646 us (0.946)
  waiting for transfers between devices: 461 us -> 407 us
  starting transfers between devices: 69.4 us -> 84.2 us
  other arithmetic: 21.3 us -> 32.3 us
    psum x1 -> x0, waiting for transfers between devices: 187 us -> none  [spread_2(): return lax.psum(jnp.where(mine, shard, jnp.zeros_like(shard)), axis)]
    all_gather x0 -> x2, waiting for transfers between devices: none -> 122 us  [spread_2(): lax.all_gather(jnp.where(mine, shard, jnp.zeros_like(shard)), axis)]
    reduce_sum x0 -> x2, other arithmetic: none -> 13.8 us  [spread_2(): jnp.sum(lax.all_gather(jnp.where(mine, shard, jnp.zeros_like(shard)), axi...]
    all_to_all x1, starting transfers between devices: 5.62 us -> 16.8 us  [body(): lax.all_to_all(value_send, 'seq', split_axis=0, concat_axis=0, tiled=True)]
    all_to_all x1, waiting for transfers between devices: 37.8 us -> 48.7 us  [body(): lax.all_to_all(key_send, 'seq', split_axis=0, concat_axis=0, tiled=True)]
  transfers between devices with their start and end apart: 18 -> 19, of which waited for: 12 -> 15; matrix products, arithmetic and copies ran while one was open for 17% -> 18% of each run, Pallas kernels for 0% -> 0%
where the time goes in v1:
time: 646 us; the launch traced here: 644 us
  waiting for transfers between devices  407 us (63%)
  starting transfers between devices  84.2 us (13%)
  local copies, waits for them, and re-layouts  75.9 us (12%)
  other arithmetic  32.3 us (5%)
  matrix products  24.8 us (4%)
  between operations  19.9 us (3%)
    psum x1, waiting for transfers between devices, body(): sum_keys, sum_values = lax.psum((far_keys, far_values), 'seq')  187 us
    all_gather x2, waiting for transfers between devices, spread_2(): lax.all_gather(jnp.where(mine, shard, jnp.zeros_like(shard)), axis)  122 us
    all_to_all x1, waiting for transfers between devices, body(): lax.all_to_all(key_send, 'seq', split_axis=0, concat_axis=0, tiled=True)  48.7 us
    dot_general x20, matrix products, product(): jnp.einsum(formula, former, latter, preferred_element_type=jnp.float32)  24.8 us
    all_to_all x1, starting transfers between devices, body(): lax.all_to_all(value_send, 'seq', split_axis=0, concat_axis=0, tiled=True)  16.8 us
    all_to_all x1, waiting for transfers between devices, body(): lax.all_to_all(values_box, 'seq', split_axis=0, concat_axis=0, tiled=True)  15.8 us
    reduce_sum x2, other arithmetic, spread_2(): jnp.sum(lax.all_gather(jnp.where(mine, shard, jnp.zeros_like(shard)), axi...  13.8 us
  transfers between devices with their start and end apart: 19, of which 15 were waited for; matrix products, arithmetic and copies ran while one was open for 18% of the time, Pallas kernels for 0%

profile of v1, /device:TPU:2, one launch (start us, length us, event | category | flops | bytes accessed | tf_op | source)
XLA Modules:
  0.0 643.7 jit_solution(5472697509527360191)
XLA Ops:
  7.2 1.7 copy.548
  8.9 4.5 all-to-all-start
  13.3 1.7 copy.547
  15.0 5.0 all-to-all-done
  20.0 3.5 all-to-all-start.1
  32.7 4.0 all-to-all-start.2
  40.1 2.3 gather_fusion
  43.4 3.8 all-to-all-start.6
  47.1 4.1 broadcast_select_fusion
  51.2 2.6 all-to-all-done.6
  53.8 12.2 %all-to-all-start.3 = ((bf16[64,2,64,128]{3,2,1,0:T(8,128)(2,1)}), bf16[64,2,64,128]{3,2,1,0:T(8,128)(2,1)}, u32[]{:S(2)}, u32[]{:S(2)}) async-start(bf16[64,2,64,128]{3,2,1,0:T(8,128)(2,1)} %get-tuple-element.89), calls=%async_computation.3 | async-start | bytes 4194304 | tf_op jit(solution)/shard_map/all_to_all | solution.py:97
  66.7 2.1 collective-permute-start
  68.7 3.5 collective-permute-start.1
  72.4 2.9 collective-permute-done
  75.3 2.3 collective-permute-done.1
  78.8 1.2 copy-done.4
  80.3 48.7 %all-to-all-done.3 = bf16[64,2,64,128]{3,2,1,0:T(8,128)(2,1)} async-done(((bf16[64,2,64,128]{3,2,1,0:T(8,128)(2,1)}), bf16[64,2,64,128]{3,2,1,0:T(8,128)(2,1)}, u32[]{:S(2)}, u32[]{:S(2)}) %all-to-all-start.3) | async-done | bytes 2097184 | tf_op jit(solution)/shard_map/all_to_all | solution.py:97
  129.0 16.8 %all-to-all-start.4 = ((bf16[64,2,64,128]{3,2,1,0:T(8,128)(2,1)}), bf16[64,2,64,128]{3,2,1,0:T(8,128)(2,1)}, u32[]{:S(2)}, u32[]{:S(2)}) async-start(bf16[64,2,64,128]{3,2,1,0:T(8,128)(2,1)} %get-tuple-element.88), calls=%async_computation.4 | async-start | bytes 4194304 | tf_op jit(solution)/shard_map/all_to_all | solution.py:98
  145.8 3.4 gather_fusion.1
  149.2 1.5 convolution_bitcast_fusion.3
  150.8 20.9 %all-gather.7.cloned.1.call-done = bf16[128,1,64,8,128]{4,3,2,1,0:T(8,128)(2,1)} async-done(((bf16[2,1,64,8,128]{4,3,2,1,0:T(8,128)(2,1)}), bf16[128,1,64,8,128]{4,3,2,1,0:T(8,128)(2,1)}) %all-gather.7.cloned.1.call-update) | async-done | bytes 16777232 | tf_op jit(solution)/shard_map/all_gather | solution.py:27
  171.7 6.8 %bitcast_reduce_fusion = bf16[2,64,8,128]{3,2,1,0:T(8,128)(2,1)S(1)} fusion(bf16[64,2,64,8,128]{4,3,2,1,0:T(8,128)(2,1)} %bitcast.336), kind=kLoop, calls=%fused_computation.6 | loop fusion | flops 8257536 | bytes 17039360 | tf_op jit(solution)/shard_map/reduce_sum | solution.py:27
  179.3 100.8 %all-gather.5.cloned.1.call-done = bf16[128,1,64,8,128]{4,3,2,1,0:T(8,128)(2,1)} async-done(((bf16[2,1,64,8,128]{4,3,2,1,0:T(8,128)(2,1)}), bf16[128,1,64,8,128]{4,3,2,1,0:T(8,128)(2,1)}) %all-gather.5.cloned.1.call-update) | async-done | bytes 16777232 | tf_op jit(solution)/shard_map/all_gather | solution.py:27
  280.1 6.9 %bitcast_reduce_fusion.1 = bf16[2,64,8,128]{3,2,1,0:T(8,128)(2,1)S(1)} fusion(bf16[64,2,64,8,128]{4,3,2,1,0:T(8,128)(2,1)} %bitcast.337), kind=kLoop, calls=%fused_computation.7 | loop fusion | flops 8257536 | bytes 17039360 | tf_op jit(solution)/shard_map/reduce_sum | solution.py:27
  289.0 1.2 fusion.4
  290.3 1.3 fusion.16
  291.5 1.3 copy-done.6
  292.9 1.3 convolution_convert_fusion
  294.2 1.9 broadcast_in_dim.44.clone
  296.0 7.5 %scatter_fusion.1 = bf16[64,2,64,128]{3,2,1,0:T(8,128)(2,1)} fusion(bf16[64,2,64,128]{3,2,1,0:T(8,128)(2,1)} %broadcast_in_dim.44.clone, s32[48]{0:T(128)S(1)} %get-tuple-element.90, bf16[48,64,128]{2,1,0:T(8,128)(2,1)} %bitcast.363), kind=kCustom, calls=%fused_computation.5 | custom fusion | bytes 2359680 | tf_op jit(solution)/shard_map/scatter | solution.py:195
  303.5 5.1 copy.378
  308.7 7.8 %all-to-all-start.10 = ((bf16[64,2,64,128]{3,1,2,0:T(2,128)(2,1)}), bf16[64,2,64,128]{3,1,2,0:T(2,128)(2,1)}, u32[]{:S(2)}, u32[]{:S(2)}) async-start(bf16[64,2,64,128]{3,1,2,0:T(2,128)(2,1)} %copy.378), calls=%async_computation.10 | async-start | bytes 4194304 | tf_op jit(solution)/shard_map/all_to_all | solution.py:198
  317.4 2.7 slice_bitcast_fusion
  320.2 1.5 convolution_bitcast_fusion.2
  321.7 3.3 gather_fusion.3
  325.0 1.6 convolution_bitcast_fusion.1
  331.1 1.6 fusion.2
  332.8 1.3 copy-done.8
  334.4 2.0 broadcast_in_dim.44.clone.1
  336.4 6.8 %scatter_fusion = bf16[64,2,64,128]{3,2,1,0:T(8,128)(2,1)} fusion(bf16[64,2,64,128]{3,2,1,0:T(8,128)(2,1)} %broadcast_in_dim.44.clone.1, s32[48]{0:T(128)S(1)} %get-tuple-element.90, bf16[48,64,128]{2,1,0:T(8,128)(2,1)S(1)} %bitcast.362), kind=kCustom, calls=%fused_computation.4 | custom fusion | bytes 2359680 | tf_op jit(solution)/shard_map/scatter | solution.py:194
  343.2 5.3 copy.371
  350.3 1.5 multiply_bitcast_fusion
  351.8 15.8 %all-to-all-done.10 = bf16[64,2,64,128]{3,1,2,0:T(2,128)(2,1)} async-done(((bf16[64,2,64,128]{3,1,2,0:T(2,128)(2,1)}), bf16[64,2,64,128]{3,1,2,0:T(2,128)(2,1)}, u32[]{:S(2)}, u32[]{:S(2)}) %all-to-all-start.10) | async-done | bytes 2097184 | tf_op jit(solution)/shard_map/all_to_all | solution.py:198
  367.7 5.6 all-to-all-start.8
  375.2 1.7 fusion.96
  378.2 2.1 convert_element_type.83
  380.3 1.9 fusion.103
  382.2 2.0 collective-permute-start.2
  384.3 3.8 collective-permute-start.3
  388.1 1.8 convolution_bitcast_fusion.11
  390.9 2.1 convolution_bitcast_fusion.7
  395.0 1.3 slice.300
  397.5 1.4 maximum_convert_fusion
  400.8 186.9 %all-reduce.6.cloned.1.call-done = (f32[2,64,8,128]{3,1,2,0:T(8,128)}, f32[2,64,8,128]{3,1,2,0:T(8,128)}) async-done(((f32[2,64,8,128]{3,1,2,0:T(8,128)}, f32[2,64,8,128]{3,1,2,0:T(8,128)}), (f32[2,64,8,128]{3,1,2,0:T(8,128)}, f32[2,64,8,128]{3,1,2,0:T(8,128)})) %all-reduce.6.cloned.1.call-update) | async-done | bytes 1048592 | tf_op jit(solution)/shard_map/psum | solution.py:177
  591.4 3.9 fusion.5
  595.3 4.3 all-to-all-start.5
  599.6 3.9 fusion.7
  603.5 2.8 all-to-all-done.5
  606.3 3.4 all-to-all-start.7
  611.1 5.3 all-to-all-done.7
  616.3 3.4 all-to-all-start.11
  620.7 5.6 all-to-all-done.11
  626.4 3.4 all-to-all-start.9
  632.0 4.5 all-to-all-done.9
  (181 shorter events, 38.3 us)
Async XLA Ops:
  7.2 29.5 %copy-start = (s32[32,128,3]{1,0,2:T(8,128)S(1)}, s32[32,128,3]{1,0,2:T(8,128)}, u32[]{:S(2)}) copy-start(s32[32,128,3]{1,0,2:T(8,128)} %param.18) | copy-start | bytes 147460
  7.2 16.4 %copy-start.37 = (s32[2]{0:T(128)S(1)}, s32[2]{0:T(128)}, u32[]{:S(2)}) copy-start(s32[2]{0:T(128)} %param.19) | copy-start | bytes 28
  8.9 11.1 %all-to-all-start = ((bf16[32,4,1024]{2,0,1:T(8,128)(2,1)}), bf16[32,4,1024]{2,0,1:T(8,128)(2,1)S(1)}, u32[]{:S(2)}, u32[]{:S(2)}) async-start(bf16[32,4,1024]{2,0,1:T(8,128)(2,1)} %bitcast.327), calls=%async_computation | async-start | bytes 524288 | tf_op jit(solution)/shard_map/all_to_all | solution.py:43
  20.0 11.9 %copy-start.35 = (bf16[32,4096]{1,0:T(8,128)(2,1)S(1)}, bf16[32,4096]{1,0:T(8,128)(2,1)}, u32[]{:S(2)}) copy-start(bf16[32,4096]{1,0:T(8,128)(2,1)} %param.14) | copy-start | bytes 786436
  20.0 10.2 %all-to-all-start.1 = ((bf16[32,4,1024]{2,0,1:T(8,128)(2,1)}), bf16[32,4,1024]{2,0,1:T(8,128)(2,1)S(1)}, u32[]{:S(2)}, u32[]{:S(2)}) async-start(bf16[32,4,1024]{2,0,1:T(8,128)(2,1)} %bitcast.326), calls=%async_computation.1 | async-start | bytes 524288 | tf_op jit(solution)/shard_map/all_to_all | solution.py:44
  23.6 148.1 %all-gather.7.cloned.1.call-start = ((), (), s32[]{:S(2)}) async-start(), calls=%async_computation.13 | async-start | bytes 17039360 | tf_op jit(solution)/shard_map/all_gather | solution.py:27
  30.3 7.9 %copy-start.36 = (bf16[32,4096]{1,0:T(8,128)(2,1)S(1)}, bf16[32,4096]{1,0:T(8,128)(2,1)}, u32[]{:S(2)}) copy-start(bf16[32,4096]{1,0:T(8,128)(2,1)} %param.17) | copy-start | bytes 786436
  31.2 248.9 %all-gather.5.cloned.1.call-start = ((), (), s32[]{:S(2)}) async-start(), calls=%async_computation.12 | async-start | bytes 17039360 | tf_op jit(solution)/shard_map/all_gather | solution.py:27
  32.7 10.7 %all-to-all-start.2 = ((bf16[32,4,1024]{2,0,1:T(8,128)(2,1)}), bf16[32,4,1024]{2,0,1:T(8,128)(2,1)S(1)}, u32[]{:S(2)}, u32[]{:S(2)}) async-start(bf16[32,4,1024]{2,0,1:T(8,128)(2,1)} %bitcast.325), calls=%async_computation.2 | async-start | bytes 524288 | tf_op jit(solution)/shard_map/all_to_all | solution.py:42
  43.4 10.4 %all-to-all-start.6 = ((bf16[32,4,1024]{2,0,1:T(8,128)(2,1)}), bf16[32,4,1024]{2,0,1:T(8,128)(2,1)S(1)}, u32[]{:S(2)}, u32[]{:S(2)}) async-start(bf16[32,4,1024]{2,0,1:T(8,128)(2,1)} %bitcast.324), calls=%async_computation.6 | async-start | bytes 524288 | tf_op jit(solution)/shard_map/all_to_all | solution.py:45
  53.8 75.2 %all-to-all-start.3 = ((bf16[64,2,64,128]{3,2,1,0:T(8,128)(2,1)}), bf16[64,2,64,128]{3,2,1,0:T(8,128)(2,1)}, u32[]{:S(2)}, u32[]{:S(2)}) async-start(bf16[64,2,64,128]{3,2,1,0:T(8,128)(2,1)} %get-tuple-element.89), calls=%async_computation.3 | async-start | bytes 4194304 | tf_op jit(solution)/shard_map/all_to_all | solution.py:97
  66.6 8.6 %copy-start.33 = (bf16[16,8,8,128]{3,2,1,0:T(8,128)(2,1)}, bf16[16,8,8,128]{3,2,1,0:T(8,128)(2,1)S(1)}, u32[]{:S(2)}) copy-start(bf16[16,8,8,128]{3,2,1,0:T(8,128)(2,1)S(1)} %copy.461) | copy-start | bytes 786436
  66.7 8.6 %collective-permute-start = (bf16[2,64,1024]{2,1,0:T(8,128)(2,1)S(1)}, bf16[2,64,1024]{2,1,0:T(8,128)(2,1)S(1)}, u32[]{:S(2)}, u32[]{:S(2)}) collective-permute-start(bf16[2,64,1024]{2,1,0:T(8,128)(2,1)S(1)} %get-tuple-element.84), channel_id=1, source_target_pairs={{0,4},{4,8},{8,12},{12,16},{16,20},{20,24},{24,28},{28,32},{32,36}... | collective-permute-start | bytes 786440 | tf_op jit(solution)/shard_map/ppermute | solution.py:19
  68.7 8.8 %collective-permute-start.1 = (bf16[2,64,1024]{2,1,0:T(8,128)(2,1)S(1)}, bf16[2,64,1024]{2,1,0:T(8,128)(2,1)S(1)}, u32[]{:S(2)}, u32[]{:S(2)}) collective-permute-start(bf16[2,64,1024]{2,1,0:T(8,128)(2,1)S(1)} %get-tuple-element.85), channel_id=1, source_target_pairs={{4,0},{8,4},{12,8},{16,12},{20,16},{24,20},{28,24},{32,28},{36,32}... | collective-permute-start | bytes 786440 | tf_op jit(solution)/shard_map/ppermute | solution.py:20
  72.3 6.5 %copy-start.10 = (bf16[2,64,8,128,1]{3,2,1,0,4:T(8,128)(2,1)}, bf16[2,64,8,128,1]{3,2,1,0,4:T(8,128)(2,1)S(1)}, u32[]{:S(2)}) copy-start(bf16[2,64,8,128,1]{3,2,1,0,4:T(8,128)(2,1)S(1)} %bitcast_bitcast_fusion.1) | copy-start | bytes 786436
  72.3 5.6 copy-start.29
  78.8 1.2 copy-start.4
  129.0 179.7 %all-to-all-start.4 = ((bf16[64,2,64,128]{3,2,1,0:T(8,128)(2,1)}), bf16[64,2,64,128]{3,2,1,0:T(8,128)(2,1)}, u32[]{:S(2)}, u32[]{:S(2)}) async-start(bf16[64,2,64,128]{3,2,1,0:T(8,128)(2,1)} %get-tuple-element.88), calls=%async_computation.4 | async-start | bytes 4194304 | tf_op jit(solution)/shard_map/all_to_all | solution.py:98
  280.1 7.7 %copy-start.11 = (bf16[2,64,8,128,1]{3,2,1,0,4:T(8,128)(2,1)S(1)}, bf16[2,64,8,128,1]{3,2,1,0,4:T(8,128)(2,1)}, u32[]{:S(2)}) copy-start(bf16[2,64,8,128,1]{3,2,1,0,4:T(8,128)(2,1)} %copy-done.10) | copy-start | bytes 786436
  280.1 7.7 %copy-start.19 = (bf16[2,64,8,128]{3,1,2,0:T(8,128)(2,1)S(1)}, bf16[2,64,8,128]{3,1,2,0:T(8,128)(2,1)}, u32[]{:S(2)}) copy-start(bf16[2,64,8,128]{3,1,2,0:T(8,128)(2,1)} %copy.549) | copy-start | bytes 786436
  287.1 0.7 copy-start.22
  288.2 2.0 copy-start.2
  291.5 1.4 copy-start.6
  308.7 8.0 %copy-start.38 = (s32[5]{0:T(128)S(1)}, s32[5]{0:T(128)}, u32[]{:S(2)}) copy-start(s32[5]{0:T(128)} %constant.249.clone.1) | copy-start | bytes 64
  308.7 59.0 %all-to-all-start.10 = ((bf16[64,2,64,128]{3,1,2,0:T(2,128)(2,1)}), bf16[64,2,64,128]{3,1,2,0:T(2,128)(2,1)}, u32[]{:S(2)}, u32[]{:S(2)}) async-start(bf16[64,2,64,128]{3,1,2,0:T(2,128)(2,1)} %copy.378), calls=%async_computation.10 | async-start | bytes 4194304 | tf_op jit(solution)/shard_map/all_to_all | solution.py:198
  316.7 3.4 copy-start.5
  325.0 1.8 copy-start.7
  326.9 1.3 copy-start.18
  326.9 1.7 copy-start.28
  327.0 2.0 copy-start.16
  328.1 1.0 copy-start.20
  328.1 1.1 copy-start.23
  328.1 1.2 copy-start.30
  329.3 1.5 copy-start.3
  329.3 1.8 copy-start.25
  331.1 3.0 copy-start.12
  332.8 1.3 copy-start.8
  343.2 5.3 copy-start.9
  348.5 1.9 copy-start.13
  349.5 0.9 copy-start.15
  351.8 21.5 %copy-start.17 = (bf16[8,2,64,3,64]{2,4,3,1,0:T(8,128)(2,1)S(1)}, bf16[8,2,64,3,64]{2,4,3,1,0:T(8,128)(2,1)}, u32[]{:S(2)}) copy-start(bf16[8,2,64,3,64]{2,4,3,1,0:T(8,128)(2,1)} %copy-done.16) | copy-start | bytes 1179652
  367.7 227.6 %all-to-all-start.8 = ((bf16[64,2,64,128]{3,1,2,0:T(2,128)(2,1)}), bf16[64,2,64,128]{3,1,2,0:T(2,128)(2,1)}, u32[]{:S(2)}, u32[]{:S(2)}) async-start(bf16[64,2,64,128]{3,1,2,0:T(2,128)(2,1)} %copy.371), calls=%async_computation.8 | async-start | bytes 4194304 | tf_op jit(solution)/shard_map/all_to_all | solution.py:197
  373.3 214.4 %all-reduce.6.cloned.1.call-start = ((), (), s32[]{:S(2)}) async-start(), calls=%async_computation.14 | async-start | bytes 2097152 | tf_op jit(solution)/shard_map/psum | solution.py:177
  373.4 1.4 copy-start.26
  378.2 11.8 %copy-start.14 = (bf16[48,64,128]{2,1,0:T(8,128)(2,1)S(1)}, bf16[48,64,128]{2,1,0:T(8,128)(2,1)}, u32[]{:S(2)}) copy-start(bf16[48,64,128]{2,1,0:T(8,128)(2,1)} %gather_fusion.1) | copy-start | bytes 2359300
  380.3 9.7 %copy-start.27 = (bf16[8,2,64,3,64]{2,4,3,1,0:T(8,128)(2,1)S(1)}, bf16[8,2,64,3,64]{2,4,3,1,0:T(8,128)(2,1)}, u32[]{:S(2)}) copy-start(bf16[8,2,64,3,64]{2,4,3,1,0:T(8,128)(2,1)} %get-tuple-element.66) | copy-start | bytes 1179652
  382.2 15.2 %collective-permute-start.2 = (bf16[2,64,1024]{2,1,0:T(8,128)(2,1)}, bf16[2,64,1024]{2,1,0:T(8,128)(2,1)}, u32[]{:S(2)}, u32[]{:S(2)}) collective-permute-start(bf16[2,64,1024]{2,1,0:T(8,128)(2,1)} %get-tuple-element.82), channel_id=1, source_target_pairs={{0,4},{4,8},{8,12},{12,16},{16,20},{20,24},{24,28},{28,32},{32,36}... | collective-permute-start | bytes 786440 | tf_op jit(solution)/shard_map/ppermute | solution.py:19
  384.3 13.2 %collective-permute-start.3 = (bf16[2,64,1024]{2,1,0:T(8,128)(2,1)}, bf16[2,64,1024]{2,1,0:T(8,128)(2,1)}, u32[]{:S(2)}, u32[]{:S(2)}) collective-permute-start(bf16[2,64,1024]{2,1,0:T(8,128)(2,1)} %get-tuple-element.83), channel_id=1, source_target_pairs={{4,0},{8,4},{12,8},{16,12},{20,16},{24,20},{28,24},{32,28},{36,32}... | collective-permute-start | bytes 786440 | tf_op jit(solution)/shard_map/ppermute | solution.py:20
  388.1 2.3 copy-start.21
  388.1 2.3 copy-start.24
  390.0 1.0 copy-start.31
  390.4 2.6 copy-start.32
  393.0 3.3 copy-start.34
  595.3 11.0 %all-to-all-start.5 = ((bf16[4,32,1024]{2,1,0:T(8,128)(2,1)}), bf16[4,32,1024]{2,1,0:T(8,128)(2,1)S(1)}, u32[]{:S(2)}, u32[]{:S(2)}) async-start(bf16[4,32,1024]{2,1,0:T(8,128)(2,1)} %all_to_all.127), calls=%async_computation.5 | async-start | bytes 524288 | tf_op jit(solution)/shard_map/all_to_all | solution.py:219
  606.3 10.1 %all-to-all-start.7 = ((bf16[4,32,1024]{2,1,0:T(8,128)(2,1)}), bf16[4,32,1024]{2,1,0:T(8,128)(2,1)S(1)}, u32[]{:S(2)}, u32[]{:S(2)}) async-start(bf16[4,32,1024]{2,1,0:T(8,128)(2,1)} %all_to_all.134), calls=%async_computation.7 | async-start | bytes 524288 | tf_op jit(solution)/shard_map/all_to_all | solution.py:220
  610.3 26.9 %copy-start.1 = (s32[32,128,3]{1,0,2:T(8,128)S(1)}, s32[32,128,3]{1,0,2:T(8,128)}, u32[]{:S(2)}) copy-start(s32[32,128,3]{1,0,2:T(8,128)} %param.18) | copy-start | bytes 147460
  616.3 10.1 %all-to-all-start.11 = ((bf16[4,32,1024]{2,1,0:T(8,128)(2,1)}), bf16[4,32,1024]{2,1,0:T(8,128)(2,1)S(1)}, u32[]{:S(2)}, u32[]{:S(2)}) async-start(bf16[4,32,1024]{2,1,0:T(8,128)(2,1)} %all_to_all.144), calls=%async_computation.11 | async-start | bytes 524288 | tf_op jit(solution)/shard_map/all_to_all | solution.py:222
  626.4 10.1 %all-to-all-start.9 = ((bf16[4,32,1024]{2,1,0:T(8,128)(2,1)}), bf16[4,32,1024]{2,1,0:T(8,128)(2,1)S(1)}, u32[]{:S(2)}, u32[]{:S(2)}) async-start(bf16[4,32,1024]{2,1,0:T(8,128)(2,1)} %all_to_all.139), calls=%async_computation.9 | async-start | bytes 524288 | tf_op jit(solution)/shard_map/all_to_all | solution.py:221
Sparse Core Ops, SparseCore 0:
  31.3 140.3 all-gather.6
  175.0 105.0 all-gather.4
  397.6 190.1 all-reduce.5
